TPU v7x, 512 devices: a whole 4x4x16 slice. The times are simulated.
512 devices in a mesh: dp: 4 (over x), mp: 128 (over y, z, core).
Axes of the slice: x: 4, y: 4, z: 16, core: 2. Of those that a mesh axis runs over, the one named last changes fastest.
Arguments:
- inputs: bfloat16 [2048, 128, 128], P('dp', 'mp'), may hold values from -6 to 6
- out_grad: bfloat16 [2048, 128, 128], P('dp', 'mp'), may hold values from -6 to 6
- outer_in: bfloat16 [128, 128, 128], P('mp'), may hold values from -0.5 to 0.5
- inner_up: bfloat16 [128, 128, 512], P('mp'), may hold values from -0.5 to 0.5
- inner_down: bfloat16 [128, 512, 128], P('mp'), may hold values from -0.25 to 0.25
- outer_out: bfloat16 [128, 128, 128], P('mp'), may hold values from -0.5 to 0.5
Outputs:
- mixed: bfloat16 [2048, 128, 128], P('dp', 'mp')
- input_grad: bfloat16 [2048, 128, 128], P('dp', 'mp')
- outer_in_grad: float32 [128, 128, 128], P('mp')
- inner_up_grad: float32 [128, 128, 512], P('mp')
- inner_down_grad: float32 [128, 512, 128], P('mp')
- outer_out_grad: float32 [128, 128, 128], P('mp')
All inputs are finite; a program needn't handle non-finite values.
Results may differ from a plain program's by a relative error of at most 0.014.
Values may be sent and summed in bfloat16 or wider, within the bound.
A program may use at most 64 MiB of HBM per device.

v0:
```python
import jax
import jax.numpy as jnp
from jax import lax
from jax.sharding import PartitionSpec as P


def gelu_grad(pre_act, grad_hidden):
    _, pull_back = jax.vjp(jax.nn.gelu, pre_act)
    return pull_back(grad_hidden)[0]


def local(inputs, out_grad, outer_in, inner_up, inner_down, outer_out):
    first = jnp.einsum("tbk,bkj->tbj", inputs, outer_in, preferred_element_type=jnp.float32).astype(
        jnp.bfloat16
    )
    grad_down = jnp.einsum(
        "tck,cjk->tcj", out_grad, outer_out, preferred_element_type=jnp.float32
    ).astype(jnp.bfloat16)
    columns = lax.all_to_all(first, "mp", split_axis=2, concat_axis=1, tiled=True)
    pre_act = jnp.einsum("tbj,jbh->tjh", columns, inner_up, preferred_element_type=jnp.float32)
    hidden = jax.nn.gelu(pre_act).astype(jnp.bfloat16)
    down = jnp.einsum(
        "tjh,jhc->tjc", hidden, inner_down, preferred_element_type=jnp.float32
    ).astype(jnp.bfloat16)
    pre_act, hidden, down = (pre_act, hidden, down)
    columns, pre_act, hidden, down = (columns, pre_act, hidden, down)
    rows_down = lax.all_to_all(down, "mp", split_axis=2, concat_axis=1, tiled=True)
    rows_down, mixed = (
        rows_down,
        jnp.einsum("tjc,cjk->tck", rows_down, outer_out, preferred_element_type=jnp.float32).astype(
            jnp.bfloat16
        ),
    )
    grad_cols = lax.all_to_all(grad_down, "mp", split_axis=2, concat_axis=1, tiled=True)
    grad_cols, grad_hidden = (
        grad_cols,
        jnp.einsum("tcj,jhc->tjh", grad_cols, inner_down, preferred_element_type=jnp.float32),
    )
    grad_pre = gelu_grad(pre_act, grad_hidden).astype(jnp.bfloat16)
    grad_first = jnp.einsum(
        "tjh,jbh->tjb", grad_pre, inner_up, preferred_element_type=jnp.float32
    ).astype(jnp.bfloat16)
    grad_pre, grad_first = (grad_pre, grad_first)
    rows_grad = lax.all_to_all(grad_first, "mp", split_axis=2, concat_axis=1, tiled=True)
    rows_grad, input_grad = (
        rows_grad,
        jnp.einsum("tjb,bkj->tbk", rows_grad, outer_in, preferred_element_type=jnp.float32).astype(
            jnp.bfloat16
        ),
    )
    inner_up_term = jnp.einsum(
        "tbj,tjh->jbh", columns, grad_pre, preferred_element_type=jnp.float32
    )
    inner_down_term = jnp.einsum(
        "tjh,tcj->jhc", hidden, grad_cols, preferred_element_type=jnp.float32
    )
    inner_up_total, inner_down_total = (
        lax.psum(inner_up_term.astype(jnp.bfloat16), "dp").astype(jnp.float32),
        lax.psum(inner_down_term.astype(jnp.bfloat16), "dp").astype(jnp.float32),
    )
    outer_in_term = jnp.einsum(
        "tbk,tjb->bkj", inputs, rows_grad, preferred_element_type=jnp.float32
    )
    outer_out_term = jnp.einsum(
        "tjc,tck->cjk", rows_down, out_grad, preferred_element_type=jnp.float32
    )
    outer_in_total, outer_out_total = (
        lax.psum(outer_in_term.astype(jnp.bfloat16), "dp").astype(jnp.float32),
        lax.psum(outer_out_term.astype(jnp.bfloat16), "dp").astype(jnp.float32),
    )
    factor = float(inputs.shape[0] * lax.axis_size("dp")) ** (-0.5)
    return (
        mixed,
        input_grad,
        outer_in_total * factor,
        inner_up_total * factor,
        inner_down_total * factor,
        outer_out_total * factor,
    )


def solution(mesh):
    in_specs = (
        P("dp", "mp", None),
        P("dp", "mp", None),
        P("mp", None, None),
        P("mp", None, None),
        P("mp", None, None),
        P("mp", None, None),
    )
    out_specs = (
        P("dp", "mp", None),
        P("dp", "mp", None),
        P("mp", None, None),
        P("mp", None, None),
        P("mp", None, None),
        P("mp", None, None),
    )
    return jax.shard_map(local, mesh=mesh, in_specs=in_specs, out_specs=out_specs, check_vma=False)
```

profile of v0, /device:TPU:1, one launch (start us, length us, event | category | flops | bytes accessed | tf_op | source)
XLA Modules:
  0.0 217.5 jit_solution(12189555219050200174)
XLA Ops:
  7.2 1.2 fusion.4
  8.4 0.2 copy.37
  8.6 0.5 broadcast.31
  9.1 1.4 reduce
  10.5 0.7 reshape.114
  11.2 20.7 %all-to-all-start = ((bf16[128,2,256]{2,1,0:T(2,128)(2,1)}), bf16[128,2,256]{2,1,0:T(2,128)(2,1)S(1)}, u32[]{:S(2)}, u32[]{:S(2)}) async-start(bf16[128,2,256]{2,1,0:T(2,128)(2,1)} %reshape.114), calls=%async_computation | async-start | bytes 262144 | tf_op jit(solution)/shard_map/all_to_all | solution.py:19
  31.9 0.2 fusion.6
  32.1 0.2 copy.36
  32.3 1.4 reduce.2
  33.7 0.7 reshape.118
  34.4 14.9 %all-to-all-done = bf16[128,2,256]{2,1,0:T(2,128)(2,1)S(1)} async-done(((bf16[128,2,256]{2,1,0:T(2,128)(2,1)}), bf16[128,2,256]{2,1,0:T(2,128)(2,1)S(1)}, u32[]{:S(2)}, u32[]{:S(2)}) %all-to-all-start) | async-done | bytes 131104 | tf_op jit(solution)/shard_map/all_to_all | solution.py:19
  49.3 6.9 %all-to-all-start.2 = ((bf16[128,2,256]{2,1,0:T(2,128)(2,1)}), bf16[128,2,256]{2,1,0:T(2,128)(2,1)S(1)}, u32[]{:S(2)}, u32[]{:S(2)}) async-start(bf16[128,2,256]{2,1,0:T(2,128)(2,1)} %reshape.118), calls=%async_computation.2 | async-start | bytes 262144 | tf_op jit(solution)/shard_map/all_to_all | solution.py:34
  56.2 0.1 reshape.115
  56.3 0.2 copy.23
  56.5 17.2 %all-to-all-done.2 = bf16[128,2,256]{2,1,0:T(2,128)(2,1)S(1)} async-done(((bf16[128,2,256]{2,1,0:T(2,128)(2,1)}), bf16[128,2,256]{2,1,0:T(2,128)(2,1)S(1)}, u32[]{:S(2)}, u32[]{:S(2)}) %all-to-all-start.2) | async-done | bytes 131104 | tf_op jit(solution)/shard_map/all_to_all | solution.py:34
  73.7 0.1 reshape.119
  73.8 0.2 copy.27
  74.0 0.5 multiply_convert_fusion
  74.5 0.4 copy-done.6
  74.9 0.8 fusion.17
  75.7 0.3 fusion.1
  76.0 0.2 copy.28
  76.2 1.4 reduce.3
  77.6 0.7 reshape.120
  78.3 6.9 %all-to-all-start.3 = ((bf16[128,2,256]{2,1,0:T(2,128)(2,1)}), bf16[128,2,256]{2,1,0:T(2,128)(2,1)S(1)}, u32[]{:S(2)}, u32[]{:S(2)}) async-start(bf16[128,2,256]{2,1,0:T(2,128)(2,1)} %reshape.120), calls=%async_computation.3 | async-start | bytes 262144 | tf_op jit(solution)/shard_map/all_to_all | solution.py:44
  85.3 0.2 all-reduce.7.cloned.1.call-start
  85.5 0.9 fusion.2
  86.4 1.0 fusion.3
  87.4 0.3 fusion
  87.7 0.2 copy.24
  87.9 1.4 reduce.1
  89.3 0.7 reshape.116
  90.0 12.7 %all-to-all-done.3 = bf16[128,2,256]{2,1,0:T(2,128)(2,1)S(1)} async-done(((bf16[128,2,256]{2,1,0:T(2,128)(2,1)}), bf16[128,2,256]{2,1,0:T(2,128)(2,1)S(1)}, u32[]{:S(2)}, u32[]{:S(2)}) %all-to-all-start.3) | async-done | bytes 131104 | tf_op jit(solution)/shard_map/all_to_all | solution.py:44
  102.8 6.9 %all-to-all-start.1 = ((bf16[128,2,256]{2,1,0:T(2,128)(2,1)}), bf16[128,2,256]{2,1,0:T(2,128)(2,1)S(1)}, u32[]{:S(2)}, u32[]{:S(2)}) async-start(bf16[128,2,256]{2,1,0:T(2,128)(2,1)} %reshape.116), calls=%async_computation.1 | async-start | bytes 262144 | tf_op jit(solution)/shard_map/all_to_all | solution.py:27
  109.8 35.4 %all-reduce.7.cloned.1.call-done = (bf16[1,128,512]{2,1,0:T(8,128)(2,1)}, bf16[1,512,128]{2,1,0:T(8,128)(2,1)}) async-done(((bf16[1,128,512]{2,1,0:T(8,128)(2,1)}, bf16[1,512,128]{2,1,0:T(8,128)(2,1)}), (bf16[1,128,512]{2,1,0:T(8,128)(2,1)}, bf16[1,512,128]{2,1,0:T(8,128)(2,1)})) %all-reduce.7.cloned.1.call-update) | async-done | bytes 262160 | tf_op jit(solution)/shard_map/psum | solution.py:58
  145.1 1.7 convert_multiply_fusion.1
  146.8 0.7 convert_multiply_fusion
  147.7 0.2 copy.29
  147.8 0.6 copy-done.4
  148.4 0.8 fusion.7
  149.3 0.8 fusion.8
  150.3 0.2 copy.25
  150.4 0.9 fusion.9
  151.3 0.8 fusion.5
  152.2 56.3 %all-reduce.5.cloned.1.call-done = (bf16[1,128,128]{1,2,0:T(8,128)(2,1)}, bf16[1,128,128]{1,2,0:T(8,128)(2,1)}) async-done(((bf16[1,128,128]{1,2,0:T(8,128)(2,1)}, bf16[1,128,128]{1,2,0:T(8,128)(2,1)}), (bf16[1,128,128]{1,2,0:T(8,128)(2,1)}, bf16[1,128,128]{1,2,0:T(8,128)(2,1)})) %all-reduce.5.cloned.1.call-update) | async-done | bytes 65552 | tf_op jit(solution)/shard_map/psum | solution.py:68
  208.5 0.8 convert_multiply_fusion.2
  209.2 0.7 copy.32
  210.0 0.7 copy.31
  (18 shorter events, 0.4 us)
Async XLA Ops:
  7.2 66.8 %copy-start = (bf16[1,128,512]{2,1,0:T(8,128)(2,1)S(1)}, bf16[1,128,512]{2,1,0:T(8,128)(2,1)}, u32[]{:S(2)}) copy-start(bf16[1,128,512]{2,1,0:T(8,128)(2,1)} %param.9) | copy-start | bytes 393220
  11.2 20.7 %copy-start.2 = (bf16[512,1,128]{2,0,1:T(8,128)(2,1)S(1)}, bf16[512,1,128]{2,0,1:T(8,128)(2,1)}, u32[]{:S(2)}) copy-start(bf16[512,1,128]{2,0,1:T(8,128)(2,1)} %param.7) | copy-start | bytes 393220
  11.2 20.7 %copy-start.5 = (bf16[1,128,128]{2,1,0:T(8,128)(2,1)S(1)}, bf16[1,128,128]{2,1,0:T(8,128)(2,1)}, u32[]{:S(2)}) copy-start(bf16[1,128,128]{2,1,0:T(8,128)(2,1)} %param.11) | copy-start | bytes 98308
  11.2 38.1 %all-to-all-start = ((bf16[128,2,256]{2,1,0:T(2,128)(2,1)}), bf16[128,2,256]{2,1,0:T(2,128)(2,1)S(1)}, u32[]{:S(2)}, u32[]{:S(2)}) async-start(bf16[128,2,256]{2,1,0:T(2,128)(2,1)} %reshape.114), calls=%async_computation | async-start | bytes 262144 | tf_op jit(solution)/shard_map/all_to_all | solution.py:19
  49.3 24.4 %all-to-all-start.2 = ((bf16[128,2,256]{2,1,0:T(2,128)(2,1)}), bf16[128,2,256]{2,1,0:T(2,128)(2,1)S(1)}, u32[]{:S(2)}, u32[]{:S(2)}) async-start(bf16[128,2,256]{2,1,0:T(2,128)(2,1)} %reshape.118), calls=%async_computation.2 | async-start | bytes 262144 | tf_op jit(solution)/shard_map/all_to_all | solution.py:34
  74.0 0.9 copy-start.6
  78.3 24.4 %all-to-all-start.3 = ((bf16[128,2,256]{2,1,0:T(2,128)(2,1)}), bf16[128,2,256]{2,1,0:T(2,128)(2,1)S(1)}, u32[]{:S(2)}, u32[]{:S(2)}) async-start(bf16[128,2,256]{2,1,0:T(2,128)(2,1)} %reshape.120), calls=%async_computation.3 | async-start | bytes 262144 | tf_op jit(solution)/shard_map/all_to_all | solution.py:44
  85.3 59.9 %all-reduce.7.cloned.1.call-start = ((), (), s32[]{:S(2)}) async-start(), calls=%async_computation.5 | async-start | bytes 524288 | tf_op jit(solution)/shard_map/psum | solution.py:58
  102.8 47.4 %all-to-all-start.1 = ((bf16[128,2,256]{2,1,0:T(2,128)(2,1)}), bf16[128,2,256]{2,1,0:T(2,128)(2,1)S(1)}, u32[]{:S(2)}, u32[]{:S(2)}) async-start(bf16[128,2,256]{2,1,0:T(2,128)(2,1)} %reshape.116), calls=%async_computation.1 | async-start | bytes 262144 | tf_op jit(solution)/shard_map/all_to_all | solution.py:27
  109.7 98.8 %all-reduce.5.cloned.1.call-start = ((), (), s32[]{:S(2)}) async-start(), calls=%async_computation.4 | async-start | bytes 131072 | tf_op jit(solution)/shard_map/psum | solution.py:68
  145.1 1.7 copy-start.3
  147.6 0.8 copy-start.4
  148.4 0.9 copy-start.1
Sparse Core Ops, SparseCore 0:
  89.1 56.0 all-reduce.6
  151.4 56.9 all-reduce.4
where the time goes:
time: 219 us; the launch traced here: 218 us
  waiting for transfers between devices  137 us (63%)
  starting transfers between devices  41.7 us (19%)
  between operations  14.2 us (6%)
  other arithmetic  8.8 us (4%)
  matrix products  8.49 us (4%)
  local copies, waits for them, and re-layouts  7.73 us (4%)
    psum x1, waiting for transfers between devices, local(): lax.psum(outer_in_term.astype(jnp.bfloat16), 'dp').astype(jnp.float32)  56.3 us
    psum x1, waiting for transfers between devices, local(): lax.psum(inner_up_term.astype(jnp.bfloat16), 'dp').astype(jnp.float32)  35.4 us
    all_to_all x1, starting transfers between devices, local(): lax.all_to_all(first, 'mp', split_axis=2, concat_axis=1, tiled=True)  20.7 us
    all_to_all x1, waiting for transfers between devices, local(): lax.all_to_all(grad_down, 'mp', split_axis=2, concat_axis=1, tiled=True)  17.2 us
    all_to_all x1, waiting for transfers between devices, local(): lax.all_to_all(first, 'mp', split_axis=2, concat_axis=1, tiled=True)  14.9 us
    all_to_all x1, waiting for transfers between devices, local(): lax.all_to_all(grad_first, 'mp', split_axis=2, concat_axis=1, tiled=True)  12.7 us
    all_to_all x1, starting transfers between devices, local(): lax.all_to_all(down, 'mp', split_axis=2, concat_axis=1, tiled=True)  6.93 us
    all_to_all x1, starting transfers between devices, local(): lax.all_to_all(grad_down, 'mp', split_axis=2, concat_axis=1, tiled=True)  6.92 us
  transfers between devices with their start and end apart: 6, of which 5 were waited for; matrix products, arithmetic and copies ran while one was open for 6% of the time, Pallas kernels for 0%

commit v1 on v0

v1 whole, which is shorter than its diff:
```python
import functools

import jax
import jax.numpy as jnp
from jax import lax
from jax.experimental import pallas as pl
from jax.experimental.pallas import tpu as pltpu
from jax.sharding import PartitionSpec as P

BF = jnp.bfloat16
F32 = jnp.float32
MESH = pl.DeviceIdType.MESH
C0 = 0.7978845608028654
C1 = 0.044715


def dot(a, b, ca, cb):
    return lax.dot_general(a, b, (((ca,), (cb,)), ((), ())), preferred_element_type=F32)


def remote(src, dst, send, recv, where):
    return pltpu.make_async_remote_copy(
        src_ref=src, dst_ref=dst, send_sem=send, recv_sem=recv, device_id=where, device_id_type=MESH
    )


def kernel(
    n,
    nd,
    factor,
    x_hbm,
    g_hbm,
    w1_hbm,
    u_hbm,
    d_hbm,
    w2_hbm,
    mixed_ref,
    igrad_ref,
    w1g_ref,
    ug_ref,
    dg_ref,
    w2g_ref,
    x_ref,
    g_ref,
    w1_ref,
    u_ref,
    d_ref,
    w2_ref,
    ut_ref,
    dt_ref,
    s1,
    s2,
    s3,
    s4,
    r1,
    r2,
    r3,
    r4,
    col_ref,
    gcol_ref,
    slope_ref,
    hid_ref,
    gp_ref,
    mid_ref,
    tu,
    td,
    ru,
    rd,
    au,
    ad,
    t_oo,
    r_oo,
    t_oi,
    r_oi,
    load_sem,
    send_sem,
    recv_sem,
    xsend_sem,
    xrecv_sem,
):
    m = lax.axis_index("mp")
    p = lax.axis_index("dp")
    loads = [
        pltpu.make_async_copy(src, dst, load_sem.at[i])
        for i, (src, dst) in enumerate(
            (
                (x_hbm, x_ref),
                (w1_hbm, w1_ref),
                (g_hbm, g_ref),
                (w2_hbm, w2_ref),
                (u_hbm, u_ref),
                (d_hbm, d_ref),
            )
        )
    ]
    for c in loads:
        c.start()

    barrier = pltpu.get_barrier_semaphore()

    @pl.loop(1, n)
    def _(i):
        pl.semaphore_signal(barrier, inc=1, device_id={"mp": (m + i) % n}, device_id_type=MESH)

    @pl.loop(1, nd)
    def _(i):
        pl.semaphore_signal(barrier, inc=1, device_id={"dp": (p + i) % nd}, device_id_type=MESH)

    def send_all(e, src, dst):
        @pl.loop(1, n)
        def _(i):
            to = (m + i) % n
            remote(src.at[to], dst.at[m], send_sem.at[e], recv_sem.at[e], {"mp": to}).start()

        dst[m] = src[m]

    def whole(e, src, dst):
        part = pl.ds(0, n - 1)
        return remote(
            src.at[part], dst.at[part], send_sem.at[e], recv_sem.at[e], {"mp": (m + 1) % n}
        )

    def send_dp(e, src, dst, cut):
        for i in range(1, nd):
            to = (p + i) % nd
            remote(
                src.at[to] if cut else src, dst.at[p], xsend_sem.at[e], xrecv_sem.at[e], {"dp": to}
            ).start()

    def whole_dp(e, dst):
        part = pl.ds(0, nd - 1)
        return remote(
            dst.at[part], dst.at[part], xsend_sem.at[e], xrecv_sem.at[e], {"dp": (p + 1) % nd}
        )

    tokens = x_ref.shape[0]
    blocks = (n, tokens // 128, 128)
    flat = (n, tokens)

    loads[0].wait()
    loads[1].wait()
    s1[...] = dot(w1_ref[...], x_ref[...], 0, 1).astype(BF).reshape(blocks)
    loads[2].wait()
    loads[3].wait()
    s2[...] = dot(w2_ref[...], g_ref[...], 1, 1).astype(BF).reshape(blocks)
    loads[4].wait()
    loads[5].wait()
    ut_ref[...] = u_ref[...].T
    dt_ref[...] = d_ref[...].T

    pl.semaphore_wait(barrier, n - 1 + nd - 1)
    send_all(0, s1, r1)
    send_all(1, s2, r2)

    half = tokens // 2
    whole(0, s1, r1).wait_recv()
    col_ref[...] = r1[...].reshape(flat)
    for q in range(2):
        cols = pl.ds(q * half, half)
        a = dot(ut_ref[...], col_ref[:, cols], 1, 0)
        sq = a * a
        th = jnp.tanh(C0 * (a + C1 * (a * sq)))
        up = 0.5 * (1.0 + th)
        hid = (a * up).astype(BF)
        hid_ref[:, cols] = hid
        slope_ref[:, cols] = up + (0.5 * a) * (1.0 - th * th) * (C0 + (3.0 * C0 * C1) * sq)
        mid_ref[:, cols] = dot(dt_ref[...], hid, 1, 0).astype(BF)
    s3[...] = mid_ref[...].reshape(blocks)
    send_all(2, s3, r3)

    whole(1, s2, r2).wait_recv()
    gcol_ref[...] = r2[...].reshape(flat)
    for q in range(2):
        cols = pl.ds(q * half, half)
        gh = dot(d_ref[...], gcol_ref[:, cols], 1, 0)
        gp = (gh * slope_ref[:, cols]).astype(BF)
        gp_ref[:, cols] = gp
        mid_ref[:, cols] = dot(u_ref[...], gp, 1, 0).astype(BF)
    s4[...] = mid_ref[...].reshape(blocks)
    send_all(3, s4, r4)

    tu[...] = dot(col_ref[...], gp_ref[...], 1, 1).astype(BF).reshape(tu.shape)
    td[...] = dot(hid_ref[...], gcol_ref[...], 1, 1).astype(BF).reshape(td.shape)
    send_dp(0, tu, ru, True)
    send_dp(1, td, rd, True)
    ru[p] = tu[p]
    rd[p] = td[p]

    whole(2, s3, r3).wait_recv()
    rows = r3[...].reshape(flat)
    t_oo[...] = dot(rows, g_ref[...], 1, 0).astype(BF)
    send_dp(2, t_oo, r_oo, False)
    r_oo[p] = t_oo[...]
    mixed_ref[...] = dot(rows, w2_ref[...], 0, 0).astype(BF)

    def added(r):
        total = r[0].astype(F32)
        for i in range(1, nd):
            total += r[i].astype(F32)
        return total

    whole_dp(0, ru).wait()
    au[p] = added(ru).astype(BF)
    whole_dp(1, rd).wait()
    ad[p] = added(rd).astype(BF)
    send_dp(3, au.at[p], au, False)
    send_dp(4, ad.at[p], ad, False)

    whole(3, s4, r4).wait_recv()
    rows = r4[...].reshape(flat)
    t_oi[...] = dot(x_ref[...], rows, 0, 1).astype(BF)
    send_dp(5, t_oi, r_oi, False)
    r_oi[p] = t_oi[...]
    igrad_ref[...] = dot(rows, w1_ref[...], 0, 1).astype(BF)

    whole_dp(3, au).wait()
    whole_dp(4, ad).wait()
    ug_ref[...] = au[...].astype(F32).reshape(ug_ref.shape) * factor
    dg_ref[...] = ad[...].astype(F32).reshape(dg_ref.shape) * factor
    whole_dp(2, r_oo).wait()
    w2g_ref[...] = added(r_oo) * factor
    whole(0, s1, r1).wait_send()
    whole(1, s2, r2).wait_send()
    whole(2, s3, r3).wait_send()
    whole(3, s4, r4).wait_send()
    whole_dp(5, r_oi).wait()
    w1g_ref[...] = added(r_oi) * factor


def local(n, nd, inputs, out_grad, outer_in, inner_up, inner_down, outer_out):
    t, _, k = inputs.shape
    h = inner_up.shape[2]
    x, g = inputs.reshape(t, k), out_grad.reshape(t, k)
    w1, u, d, w2 = outer_in[0], inner_up[0], inner_down[0], outer_out[0]
    shape = jax.ShapeDtypeStruct
    vm = pltpu.VMEM
    lanes = t // 128
    blocks = vm((n, lanes, 128), BF)
    outs = pl.pallas_call(
        functools.partial(kernel, n, nd, float(t * nd) ** -0.5),
        out_shape=(
            shape((t, k), BF),
            shape((t, k), BF),
            shape((k, n), F32),
            shape((n, h), F32),
            shape((h, n), F32),
            shape((n, k), F32),
        ),
        in_specs=[pl.BlockSpec(memory_space=pl.ANY)] * 6,
        out_specs=[pl.BlockSpec(memory_space=pltpu.VMEM)] * 6,
        scratch_shapes=[
            vm((t, k), BF),
            vm((t, k), BF),
            vm((k, n), BF),
            vm((n, h), BF),
            vm((h, n), BF),
            vm((n, k), BF),
            vm((h, n), BF),
            vm((n, h), BF),
        ]
        + [blocks] * 8
        + [
            vm((n, t), BF),
            vm((n, t), BF),
            vm((h, t), F32),
            vm((h, t), BF),
            vm((h, t), BF),
            vm((n, t), BF),
            vm((nd, n // nd, h), BF),
            vm((nd, h // nd, n), BF),
            vm((nd, n // nd, h), BF),
            vm((nd, h // nd, n), BF),
            vm((nd, n // nd, h), BF),
            vm((nd, h // nd, n), BF),
            vm((n, k), BF),
            vm((nd, n, k), BF),
            vm((k, n), BF),
            vm((nd, k, n), BF),
            pltpu.SemaphoreType.DMA((6,)),
            pltpu.SemaphoreType.DMA((4,)),
            pltpu.SemaphoreType.DMA((4,)),
            pltpu.SemaphoreType.DMA((6,)),
            pltpu.SemaphoreType.DMA((6,)),
        ],
        compiler_params=pltpu.CompilerParams(
            collective_id=0, has_side_effects=True, vmem_limit_bytes=32 * 1024 * 1024
        ),
    )(x, g, w1, u, d, w2)
    mixed, igrad, w1g, ug, dg, w2g = outs
    return (
        mixed.reshape(t, 1, k),
        igrad.reshape(t, 1, k),
        w1g[None],
        ug[None],
        dg[None],
        w2g[None],
    )


def solution(mesh):
    n, nd = mesh.shape["mp"], mesh.shape["dp"]
    specs = (
        P("dp", "mp", None),
        P("dp", "mp", None),
        P("mp", None, None),
        P("mp", None, None),
        P("mp", None, None),
        P("mp", None, None),
    )
    return jax.shard_map(
        functools.partial(local, n, nd), mesh=mesh, in_specs=specs, out_specs=specs, check_vma=False
    )
```

time: 219 us -> 64.5 us (0.29)
  waiting for transfers between devices: 137 us -> 0 us
  Pallas kernels: 0 us -> 54.4 us
  starting transfers between devices: 41.7 us -> 0 us
  between operations: 14.2 us -> 0.66 us
  other arithmetic: 8.8 us -> 0 us
  matrix products: 8.49 us -> 0 us
    psum x2 -> x0, waiting for transfers between devices: 91.7 us -> none  [the longest x1 56.3 us: local(): lax.psum(outer_in_term.astype(jnp.bfloat16), 'dp').astype(jnp.float32)]
    pallas_call x0 -> x1, Pallas kernels: none -> 54.4 us  [local(): pl.pallas_call(functools.partial(kernel, n, nd, float(t * nd) ** (-0.5)),...]
    all_to_all x4 -> x0, waiting for transfers between devices: 44.8 us -> none  [the longest x1 17.2 us: local(): lax.all_to_all(grad_down, 'mp', split_axis=2, concat_axis=1, tiled=True)]
    all_to_all x4 -> x0, starting transfers between devices: 41.5 us -> none  [the longest x1 20.7 us: local(): lax.all_to_all(first, 'mp', split_axis=2, concat_axis=1, tiled=True)]
    dot_general x12 -> x0, matrix products: 8.49 us -> none  [the longest x1 1.16 us: local(): jnp.einsum('tbk,bkj->tbj', inputs, outer_in, preferred_element_type=jnp.f...]
    unnamed x4 -> x0, other arithmetic: 5.62 us -> none
    mul x3 -> x0, other arithmetic: 3.18 us -> none  [the longest x1 1.67 us: local(): inner_up_total * factor]
    unnamed x25 -> x18, local copies, waits for them, and re-layouts: 6.21 us -> 9.1 us
  transfers between devices with their start and end apart: 6 -> 0, of which waited for: 5 -> 0; matrix products, arithmetic and copies ran while one was open for 6% -> 0% of each run, Pallas kernels for 0% -> 0%
where the time goes in v1:
time: 64.5 us; the launch traced here: 64.2 us
  Pallas kernels  54.4 us (84%)
  local copies, waits for them, and re-layouts  9.1 us (14%)
  between operations  0.66 us (1%)
    pallas_call x1, Pallas kernels, local(): pl.pallas_call(functools.partial(kernel, n, nd, float(t * nd) ** (-0.5)),...  54.4 us
    unnamed x18, local copies, waits for them, and re-layouts  9.1 us

profile of v1, /device:TPU:1, one launch (start us, length us, event | category | flops | bytes accessed | tf_op | source)
XLA Modules:
  0.0 64.2 jit_solution(1482949041613966474)
XLA Ops:
  0.6 0.0 copy-start
  0.6 0.9 %copy-done = bf16[512,1,128]{2,0,1:T(8,128)(2,1)S(1)} copy-done((bf16[512,1,128]{2,0,1:T(8,128)(2,1)S(1)}, bf16[512,1,128]{2,0,1:T(8,128)(2,1)}, u32[]{:S(2)}) %copy-start) | copy-done | bytes 131096
  1.5 0.0 copy-start.1
  1.5 0.9 %copy-done.1 = bf16[512,1,128]{2,0,1:T(8,128)(2,1)S(1)} copy-done((bf16[512,1,128]{2,0,1:T(8,128)(2,1)S(1)}, bf16[512,1,128]{2,0,1:T(8,128)(2,1)}, u32[]{:S(2)}) %copy-start.1) | copy-done | bytes 131096
  2.4 0.0 copy-start.2
  2.4 0.9 %copy-done.2 = bf16[1,128,512]{2,1,0:T(8,128)(2,1)S(1)} copy-done((bf16[1,128,512]{2,1,0:T(8,128)(2,1)S(1)}, bf16[1,128,512]{2,1,0:T(8,128)(2,1)}, u32[]{:S(2)}) %copy-start.2) | copy-done | bytes 131096
  3.3 0.0 copy-start.3
  3.4 0.9 %copy-done.3 = bf16[1,512,128]{2,1,0:T(8,128)(2,1)S(1)} copy-done((bf16[1,512,128]{2,1,0:T(8,128)(2,1)S(1)}, bf16[1,512,128]{2,1,0:T(8,128)(2,1)}, u32[]{:S(2)}) %copy-start.3) | copy-done | bytes 131096
  4.3 0.0 copy-start.4
  4.3 0.8 %copy-done.4 = bf16[1,128,128]{2,1,0:T(8,128)(2,1)S(1)} copy-done((bf16[1,128,128]{2,1,0:T(8,128)(2,1)S(1)}, bf16[1,128,128]{2,1,0:T(8,128)(2,1)}, u32[]{:S(2)}) %copy-start.4) | copy-done | bytes 32792
  5.0 0.0 copy-start.5
  5.0 0.8 %copy-done.5 = bf16[1,128,128]{2,1,0:T(8,128)(2,1)S(1)} copy-done((bf16[1,128,128]{2,1,0:T(8,128)(2,1)S(1)}, bf16[1,128,128]{2,1,0:T(8,128)(2,1)}, u32[]{:S(2)}) %copy-start.5) | copy-done | bytes 32792
  5.8 54.4 %shard_map.109 = (bf16[512,128]{1,0:T(8,128)(2,1)S(1)}, bf16[512,128]{1,0:T(8,128)(2,1)S(1)}, f32[128,128]{1,0:T(8,128)S(1)}, f32[128,512]{1,0:T(8,128)S(1)}, f3...) custom-call(bf16[512,128]{1,0:T(8,128)(2,1)S(1)} %bitcast.16, bf16[512,128]{1,0:T(8,128)(2,1)S(1)} %bitcast.17, ...), custom_call_target="tpu_custom_call" | custom-call | tf_op jit(solution)/shard_map/pallas_call | solution.py:239
  60.2 0.7 %copy.18 = bf16[512,1,128]{2,0,1:T(8,128)(2,1)} copy(bf16[512,1,128]{2,0,1:T(8,128)(2,1)S(1)} %bitcast.15) | data formatting | bytes 262144
  60.9 0.7 %copy.19 = bf16[512,1,128]{2,0,1:T(8,128)(2,1)} copy(bf16[512,1,128]{2,0,1:T(8,128)(2,1)S(1)} %bitcast.14) | data formatting | bytes 262144
  61.5 0.6 copy.20
  62.1 0.7 %copy.21 = f32[1,128,512]{2,1,0:T(8,128)} copy(f32[1,128,512]{2,1,0:T(8,128)S(1)} %bitcast.13) | data formatting | bytes 524288
  62.8 0.7 %copy.22 = f32[1,512,128]{2,1,0:T(8,128)} copy(f32[1,512,128]{2,1,0:T(8,128)S(1)} %bitcast.12) | data formatting | bytes 524288
  63.6 0.6 copy.23
Async XLA Ops:
  0.6 0.9 %copy-start = (bf16[512,1,128]{2,0,1:T(8,128)(2,1)S(1)}, bf16[512,1,128]{2,0,1:T(8,128)(2,1)}, u32[]{:S(2)}) copy-start(bf16[512,1,128]{2,0,1:T(8,128)(2,1)} %param.6) | copy-start | bytes 393220
  1.5 0.9 %copy-start.1 = (bf16[512,1,128]{2,0,1:T(8,128)(2,1)S(1)}, bf16[512,1,128]{2,0,1:T(8,128)(2,1)}, u32[]{:S(2)}) copy-start(bf16[512,1,128]{2,0,1:T(8,128)(2,1)} %param.7) | copy-start | bytes 393220
  2.4 0.9 %copy-start.2 = (bf16[1,128,512]{2,1,0:T(8,128)(2,1)S(1)}, bf16[1,128,512]{2,1,0:T(8,128)(2,1)}, u32[]{:S(2)}) copy-start(bf16[1,128,512]{2,1,0:T(8,128)(2,1)} %param.9) | copy-start | bytes 393220
  3.3 0.9 %copy-start.3 = (bf16[1,512,128]{2,1,0:T(8,128)(2,1)S(1)}, bf16[1,512,128]{2,1,0:T(8,128)(2,1)}, u32[]{:S(2)}) copy-start(bf16[1,512,128]{2,1,0:T(8,128)(2,1)} %param.10) | copy-start | bytes 393220
  4.3 0.8 %copy-start.4 = (bf16[1,128,128]{2,1,0:T(8,128)(2,1)S(1)}, bf16[1,128,128]{2,1,0:T(8,128)(2,1)}, u32[]{:S(2)}) copy-start(bf16[1,128,128]{2,1,0:T(8,128)(2,1)} %param.8) | copy-start | bytes 98308
  5.0 0.8 %copy-start.5 = (bf16[1,128,128]{2,1,0:T(8,128)(2,1)S(1)}, bf16[1,128,128]{2,1,0:T(8,128)(2,1)}, u32[]{:S(2)}) copy-start(bf16[1,128,128]{2,1,0:T(8,128)(2,1)} %param.11) | copy-start | bytes 98308

commit v2 on v1

--- a/solution.py
+++ b/solution.py
@@ -10,6 +10,7 @@
 BF = jnp.bfloat16
 F32 = jnp.float32
 MESH = pl.DeviceIdType.MESH
+DEPTH = 16
 C0 = 0.7978845608028654
 C1 = 0.044715
 
@@ -48,6 +49,7 @@
     w2_ref,
     ut_ref,
     dt_ref,
+    w1t_ref,
     s1,
     s2,
     s3,
@@ -77,6 +79,13 @@
     recv_sem,
     xsend_sem,
     xrecv_sem,
+    out_sem,
+    mixed_v,
+    igrad_v,
+    w1g_v,
+    ug_v,
+    dg_v,
+    w2g_v,
 ):
     m = lax.axis_index("mp")
     p = lax.axis_index("dp")
@@ -98,20 +107,37 @@
 
     barrier = pltpu.get_barrier_semaphore()
 
-    @pl.loop(1, n)
-    def _(i):
-        pl.semaphore_signal(barrier, inc=1, device_id={"mp": (m + i) % n}, device_id_type=MESH)
-
-    @pl.loop(1, nd)
-    def _(i):
+    plane = n // DEPTH
+    z = (m // 2) % DEPTH
+    yc = (m // (2 * DEPTH)) * 2 + m % 2
+    bases = []
+    for k in range(plane - 1, -1, -1):
+        t = (yc + k) % plane
+        bases.append((t // 2) * (2 * DEPTH) + t % 2)
+
+    def partners(act):
+        @pl.loop(0, DEPTH - 1)
+        def _(i):
+            far = (DEPTH - i) // 2
+            zt = (z + DEPTH + far * (1 - 2 * (i % 2))) % DEPTH
+            for base in bases:
+                act(base + 2 * zt)
+
+        for base in bases[:-1]:
+            act(base + 2 * z)
+
+    def greet(to):
+        pl.semaphore_signal(barrier, inc=1, device_id={"mp": to}, device_id_type=MESH)
+
+    partners(greet)
+    for i in range(1, nd):
         pl.semaphore_signal(barrier, inc=1, device_id={"dp": (p + i) % nd}, device_id_type=MESH)
 
     def send_all(e, src, dst):
-        @pl.loop(1, n)
-        def _(i):
-            to = (m + i) % n
+        def act(to):
             remote(src.at[to], dst.at[m], send_sem.at[e], recv_sem.at[e], {"mp": to}).start()
 
+        partners(act)
         dst[m] = src[m]
 
     def whole(e, src, dst):
@@ -133,6 +159,13 @@
             dst.at[part], dst.at[part], xsend_sem.at[e], xrecv_sem.at[e], {"dp": (p + 1) % nd}
         )
 
+    outs = []
+
+    def store_out(i, src, dst):
+        c = pltpu.make_async_copy(src, dst, out_sem.at[i])
+        c.start()
+        outs.append(c)
+
     tokens = x_ref.shape[0]
     blocks = (n, tokens // 128, 128)
     flat = (n, tokens)
@@ -140,17 +173,17 @@
     loads[0].wait()
     loads[1].wait()
     s1[...] = dot(w1_ref[...], x_ref[...], 0, 1).astype(BF).reshape(blocks)
+    pl.semaphore_wait(barrier, n - 1 + nd - 1)
+    send_all(0, s1, r1)
     loads[2].wait()
     loads[3].wait()
     s2[...] = dot(w2_ref[...], g_ref[...], 1, 1).astype(BF).reshape(blocks)
+    send_all(1, s2, r2)
     loads[4].wait()
     loads[5].wait()
     ut_ref[...] = u_ref[...].T
     dt_ref[...] = d_ref[...].T
-
-    pl.semaphore_wait(barrier, n - 1 + nd - 1)
-    send_all(0, s1, r1)
-    send_all(1, s2, r2)
+    w1t_ref[...] = w1_ref[...].T
 
     half = tokens // 2
     whole(0, s1, r1).wait_recv()
@@ -191,7 +224,9 @@
     t_oo[...] = dot(rows, g_ref[...], 1, 0).astype(BF)
     send_dp(2, t_oo, r_oo, False)
     r_oo[p] = t_oo[...]
-    mixed_ref[...] = dot(rows, w2_ref[...], 0, 0).astype(BF)
+    mixed_v[...] = dot(rows, w2_ref[...], 0, 0).astype(BF)
+
+    store_out(0, mixed_v, mixed_ref)
 
     def added(r):
         total = r[0].astype(F32)
@@ -206,25 +241,45 @@
     send_dp(3, au.at[p], au, False)
     send_dp(4, ad.at[p], ad, False)
 
-    whole(3, s4, r4).wait_recv()
-    rows = r4[...].reshape(flat)
-    t_oi[...] = dot(x_ref[...], rows, 0, 1).astype(BF)
-    send_dp(5, t_oi, r_oi, False)
-    r_oi[p] = t_oi[...]
-    igrad_ref[...] = dot(rows, w1_ref[...], 0, 1).astype(BF)
-
+    whole_dp(2, r_oo).wait()
+    w2g_v[...] = added(r_oo) * factor
+    store_out(5, w2g_v, w2g_ref)
     whole_dp(3, au).wait()
+    ug_v[...] = au[...].astype(F32).reshape(ug_ref.shape) * factor
+    store_out(3, ug_v, ug_ref)
     whole_dp(4, ad).wait()
-    ug_ref[...] = au[...].astype(F32).reshape(ug_ref.shape) * factor
-    dg_ref[...] = ad[...].astype(F32).reshape(dg_ref.shape) * factor
-    whole_dp(2, r_oo).wait()
-    w2g_ref[...] = added(r_oo) * factor
+    dg_v[...] = ad[...].astype(F32).reshape(dg_ref.shape) * factor
+    store_out(4, dg_v, dg_ref)
     whole(0, s1, r1).wait_send()
     whole(1, s2, r2).wait_send()
     whole(2, s3, r3).wait_send()
+
+    whole(3, s4, r4).wait_recv()
+    rows = r4[...].reshape(flat)
+    t_oi[...] = dot(rows, x_ref[...], 1, 0).astype(BF)
+    send_dp(5, t_oi, r_oi, False)
+    r_oi[p] = t_oi[...]
+    igrad_v[...] = dot(rows, w1t_ref[...], 0, 0).astype(BF)
+    store_out(1, igrad_v, igrad_ref)
     whole(3, s4, r4).wait_send()
     whole_dp(5, r_oi).wait()
-    w1g_ref[...] = added(r_oi) * factor
+    w1g_v[...] = added(r_oi).T * factor
+    store_out(2, w1g_v, w1g_ref)
+    for c in outs:
+        c.wait()
+
+
+def store(*refs):
+    src, dst, mid, sem = refs[:6], refs[6:12], refs[12:18], refs[18]
+    into = [pltpu.make_async_copy(src[i], mid[i], sem.at[i]) for i in range(6)]
+    out = [pltpu.make_async_copy(mid[i], dst[i], sem.at[6 + i]) for i in range(6)]
+    for c in into:
+        c.start()
+    for i in range(6):
+        into[i].wait()
+        out[i].start()
+    for c in out:
+        c.wait()
 
 
 def local(n, nd, inputs, out_grad, outer_in, inner_up, inner_down, outer_out):
@@ -247,7 +302,7 @@
             shape((n, k), F32),
         ),
         in_specs=[pl.BlockSpec(memory_space=pl.ANY)] * 6,
-        out_specs=[pl.BlockSpec(memory_space=pltpu.VMEM)] * 6,
+        out_specs=[pl.BlockSpec(memory_space=pl.ANY)] * 6,
         scratch_shapes=[
             vm((t, k), BF),
             vm((t, k), BF),
@@ -257,6 +312,7 @@
             vm((n, k), BF),
             vm((h, n), BF),
             vm((n, h), BF),
+            vm((n, k), BF),
         ]
         + [blocks] * 8
         + [
@@ -274,18 +330,33 @@
             vm((nd, h // nd, n), BF),
             vm((n, k), BF),
             vm((nd, n, k), BF),
-            vm((k, n), BF),
-            vm((nd, k, n), BF),
+            vm((n, k), BF),
+            vm((nd, n, k), BF),
             pltpu.SemaphoreType.DMA((6,)),
             pltpu.SemaphoreType.DMA((4,)),
             pltpu.SemaphoreType.DMA((4,)),
             pltpu.SemaphoreType.DMA((6,)),
             pltpu.SemaphoreType.DMA((6,)),
+            pltpu.SemaphoreType.DMA((6,)),
+            vm((t, k), BF),
+            vm((t, k), BF),
+            vm((k, n), F32),
+            vm((n, h), F32),
+            vm((h, n), F32),
+            vm((n, k), F32),
         ],
         compiler_params=pltpu.CompilerParams(
-            collective_id=0, has_side_effects=True, vmem_limit_bytes=32 * 1024 * 1024
+            collective_id=0, has_side_effects=True, vmem_limit_bytes=62 * 1024 * 1024
         ),
     )(x, g, w1, u, d, w2)
+    outs = pl.pallas_call(
+        store,
+        out_shape=tuple(shape(o.shape, o.dtype) for o in outs),
+        in_specs=[pl.BlockSpec(memory_space=pl.ANY)] * 6,
+        out_specs=[pl.BlockSpec(memory_space=pl.ANY)] * 6,
+        scratch_shapes=[vm(o.shape, o.dtype) for o in outs] + [pltpu.SemaphoreType.DMA((12,))],
+        compiler_params=pltpu.CompilerParams(vmem_limit_bytes=62 * 1024 * 1024),
+    )(*outs)
     mixed, igrad, w1g, ug, dg, w2g = outs
     return (
         mixed.reshape(t, 1, k),

time: 64.5 us -> 55.2 us (0.86)
  local copies, waits for them, and re-layouts: 9.1 us -> 0 us
    unnamed x18 -> x0, local copies, waits for them, and re-layouts: 9.1 us -> none
    pallas_call x0 -> x1, Pallas kernels: none -> 2.02 us  [local(): pl.pallas_call(store, out_shape=tuple((shape(o.shape, o.dtype) for o in o...]
    pallas_call x1, Pallas kernels: 54.4 us -> 52.4 us  [local(): pl.pallas_call(functools.partial(kernel, n, nd, float(t * nd) ** (-0.5)),...]
where the time goes in v2:
time: 55.2 us; the launch traced here: 55.1 us
  Pallas kernels  54.5 us (99%)
  between operations  0.64 us (1%)
    pallas_call x1, Pallas kernels, local(): pl.pallas_call(functools.partial(kernel, n, nd, float(t * nd) ** (-0.5)),...  52.4 us
    pallas_call x1, Pallas kernels, local(): pl.pallas_call(store, out_shape=tuple((shape(o.shape, o.dtype) for o in o...  2.02 us

profile of v2, /device:TPU:1, one launch (start us, length us, event | category | flops | bytes accessed | tf_op | source)
XLA Modules:
  0.0 55.1 jit_solution(18326924201117267354)
XLA Ops:
  0.6 52.4 %shard_map.109 = (bf16[512,128]{1,0:T(8,128)(2,1)}, bf16[512,128]{1,0:T(8,128)(2,1)}, f32[128,128]{1,0:T(8,128)}, f32[128,512]{1,0:T(8,128)}, f32[512,128]{1,0:T(8,128)}, /*index=5*/f32[128,128]{1,0:T(8,128)}) custom-call(bf16[512,128]{1,0:T(8,128)(2,1)} %bitcast.12, bf16[512,128]{1,0:T(8,128)(2,1)} %bitcast.13, bf16[128,128]{1,0:T(8,128)(2,1)} %bitcast.16, ...), custom_call_target="tpu_custom_call" | custom-call | tf_op jit(solution)/shard_map/pallas_call | solution.py:294
  53.1 2.0 %shard_map.110 = (bf16[512,128]{1,0:T(8,128)(2,1)}, bf16[512,128]{1,0:T(8,128)(2,1)}, f32[128,128]{1,0:T(8,128)}, f32[128,512]{1,0:T(8,128)}, f32[512,128]{1,0:T(8,128)}, /*index=5*/f32[128,128]{1,0:T(8,128)}) custom-call(bf16[512,128]{1,0:T(8,128)(2,1)} %get-tuple-element.18.refs_0_, bf16[512,128]{1,0:T(8,128)(2,1)} %get-tuple-element.19.refs_1_, ...), custom_call_target="tpu_custom_call" | custom-call | tf_op jit(solution)/shard_map/pallas_call | solution.py:352

commit v3 on v2

--- a/solution.py
+++ b/solution.py
@@ -115,16 +115,17 @@
         t = (yc + k) % plane
         bases.append((t // 2) * (2 * DEPTH) + t % 2)
 
-    def partners(act):
-        @pl.loop(0, DEPTH - 1)
+    def partners(act, lo=0, hi=DEPTH - 1):
+        @pl.loop(lo, hi)
         def _(i):
             far = (DEPTH - i) // 2
             zt = (z + DEPTH + far * (1 - 2 * (i % 2))) % DEPTH
             for base in bases:
                 act(base + 2 * zt)
 
-        for base in bases[:-1]:
-            act(base + 2 * z)
+        if hi == DEPTH - 1:
+            for base in bases[:-1]:
+                act(base + 2 * z)
 
     def greet(to):
         pl.semaphore_signal(barrier, inc=1, device_id={"mp": to}, device_id_type=MESH)
@@ -133,12 +134,13 @@
     for i in range(1, nd):
         pl.semaphore_signal(barrier, inc=1, device_id={"dp": (p + i) % nd}, device_id_type=MESH)
 
-    def send_all(e, src, dst):
+    def send_all(e, src, dst, lo=0, hi=DEPTH - 1):
         def act(to):
             remote(src.at[to], dst.at[m], send_sem.at[e], recv_sem.at[e], {"mp": to}).start()
 
-        partners(act)
-        dst[m] = src[m]
+        partners(act, lo, hi)
+        if lo == 0:
+            dst[m] = src[m]
 
     def whole(e, src, dst):
         part = pl.ds(0, n - 1)
@@ -165,6 +167,12 @@
         c = pltpu.make_async_copy(src, dst, out_sem.at[i])
         c.start()
         outs.append(c)
+
+    def added(r):
+        total = r[0].astype(F32)
+        for i in range(1, nd):
+            total += r[i].astype(F32)
+        return total
 
     tokens = x_ref.shape[0]
     blocks = (n, tokens // 128, 128)
@@ -203,21 +211,28 @@
 
     whole(1, s2, r2).wait_recv()
     gcol_ref[...] = r2[...].reshape(flat)
+    td[...] = dot(hid_ref[...], gcol_ref[...], 1, 1).astype(BF).reshape(td.shape)
+    send_dp(1, td, rd, True)
     for q in range(2):
         cols = pl.ds(q * half, half)
         gh = dot(d_ref[...], gcol_ref[:, cols], 1, 0)
         gp = (gh * slope_ref[:, cols]).astype(BF)
         gp_ref[:, cols] = gp
         mid_ref[:, cols] = dot(u_ref[...], gp, 1, 0).astype(BF)
+    tu[...] = dot(col_ref[...], gp_ref[...], 1, 1).astype(BF).reshape(tu.shape)
+    send_dp(0, tu, ru, True)
     s4[...] = mid_ref[...].reshape(blocks)
-    send_all(3, s4, r4)
-
-    tu[...] = dot(col_ref[...], gp_ref[...], 1, 1).astype(BF).reshape(tu.shape)
-    td[...] = dot(hid_ref[...], gcol_ref[...], 1, 1).astype(BF).reshape(td.shape)
-    send_dp(0, tu, ru, True)
-    send_dp(1, td, rd, True)
+    send_all(3, s4, r4, 0, 8)
     ru[p] = tu[p]
     rd[p] = td[p]
+    whole_dp(0, ru).wait()
+    au[p] = added(ru).astype(BF)
+    whole_dp(1, rd).wait()
+    ad[p] = added(rd).astype(BF)
+    send_dp(3, au.at[p], au, False)
+    send_dp(4, ad.at[p], ad, False)
+    send_all(3, s4, r4, 8)
+
 
     whole(2, s3, r3).wait_recv()
     rows = r3[...].reshape(flat)
@@ -228,18 +243,6 @@
 
     store_out(0, mixed_v, mixed_ref)
 
-    def added(r):
-        total = r[0].astype(F32)
-        for i in range(1, nd):
-            total += r[i].astype(F32)
-        return total
-
-    whole_dp(0, ru).wait()
-    au[p] = added(ru).astype(BF)
-    whole_dp(1, rd).wait()
-    ad[p] = added(rd).astype(BF)
-    send_dp(3, au.at[p], au, False)
-    send_dp(4, ad.at[p], ad, False)
 
     whole_dp(2, r_oo).wait()
     w2g_v[...] = added(r_oo) * factor

time: 55.2 us -> 53.9 us (0.976)
  Pallas kernels: 54.5 us -> 53.1 us
    pallas_call x1, Pallas kernels: 52.4 us -> 51.1 us  [local(): pl.pallas_call(functools.partial(kernel, n, nd, float(t * nd) ** (-0.5)),...]
where the time goes in v3:
time: 53.9 us; the launch traced here: 53.8 us
  Pallas kernels  53.1 us (99%)
  between operations  0.64 us (1%)
    pallas_call x1, Pallas kernels, local(): pl.pallas_call(functools.partial(kernel, n, nd, float(t * nd) ** (-0.5)),...  51.1 us
    pallas_call x1, Pallas kernels, local(): pl.pallas_call(store, out_shape=tuple((shape(o.shape, o.dtype) for o in o...  2.02 us

profile of v3, /device:TPU:1, one launch (start us, length us, event | category | flops | bytes accessed | tf_op | source)
XLA Modules:
  0.0 53.8 jit_solution(12546617716592177555)
XLA Ops:
  0.6 51.1 %shard_map.109 = (bf16[512,128]{1,0:T(8,128)(2,1)}, bf16[512,128]{1,0:T(8,128)(2,1)}, f32[128,128]{1,0:T(8,128)}, f32[128,512]{1,0:T(8,128)}, f32[512,128]{1,0:T(8,128)}, /*index=5*/f32[128,128]{1,0:T(8,128)}) custom-call(bf16[512,128]{1,0:T(8,128)(2,1)} %bitcast.12, bf16[512,128]{1,0:T(8,128)(2,1)} %bitcast.13, bf16[128,128]{1,0:T(8,128)(2,1)} %bitcast.16, ...), custom_call_target="tpu_custom_call" | custom-call | tf_op jit(solution)/shard_map/pallas_call | solution.py:297
  51.7 2.0 %shard_map.110 = (bf16[512,128]{1,0:T(8,128)(2,1)}, bf16[512,128]{1,0:T(8,128)(2,1)}, f32[128,128]{1,0:T(8,128)}, f32[128,512]{1,0:T(8,128)}, f32[512,128]{1,0:T(8,128)}, /*index=5*/f32[128,128]{1,0:T(8,128)}) custom-call(bf16[512,128]{1,0:T(8,128)(2,1)} %get-tuple-element.18.refs_0_, bf16[512,128]{1,0:T(8,128)(2,1)} %get-tuple-element.19.refs_1_, ...), custom_call_target="tpu_custom_call" | custom-call | tf_op jit(solution)/shard_map/pallas_call | solution.py:355

commit v4 on v3

--- a/solution.py
+++ b/solution.py
@@ -11,6 +11,7 @@
 F32 = jnp.float32
 MESH = pl.DeviceIdType.MESH
 DEPTH = 16
+FAR = 10
 C0 = 0.7978845608028654
 C1 = 0.044715
 
@@ -50,6 +51,8 @@
     ut_ref,
     dt_ref,
     w1t_ref,
+    rel_ref,
+    acc_ref,
     s1,
     s2,
     s3,
@@ -61,6 +64,7 @@
     col_ref,
     gcol_ref,
     slope_ref,
+    th_ref,
     hid_ref,
     gp_ref,
     mid_ref,
@@ -74,6 +78,8 @@
     r_oo,
     t_oi,
     r_oi,
+    t_oj,
+    r_oj,
     load_sem,
     send_sem,
     recv_sem,
@@ -115,17 +121,19 @@
         t = (yc + k) % plane
         bases.append((t // 2) * (2 * DEPTH) + t % 2)
 
-    def partners(act, lo=0, hi=DEPTH - 1):
-        @pl.loop(lo, hi)
+    def partners(act):
+        @pl.loop(0, DEPTH - 1)
         def _(i):
             far = (DEPTH - i) // 2
             zt = (z + DEPTH + far * (1 - 2 * (i % 2))) % DEPTH
             for base in bases:
                 act(base + 2 * zt)
 
-        if hi == DEPTH - 1:
-            for base in bases[:-1]:
-                act(base + 2 * z)
+        for base in bases[:-1]:
+            act(base + 2 * z)
+
+    steps = [(z + DEPTH + ((DEPTH - q) // 2) * (1 - 2 * (q % 2))) % DEPTH for q in range(DEPTH - 1)]
+    slot_z = steps[1 : FAR + 1] + steps[:1] + steps[FAR + 1 :] + [z]
 
     def greet(to):
         pl.semaphore_signal(barrier, inc=1, device_id={"mp": to}, device_id_type=MESH)
@@ -134,13 +142,36 @@
     for i in range(1, nd):
         pl.semaphore_signal(barrier, inc=1, device_id={"dp": (p + i) % nd}, device_id_type=MESH)
 
-    def send_all(e, src, dst, lo=0, hi=DEPTH - 1):
+    def send_all(e, src, dst):
         def act(to):
             remote(src.at[to], dst.at[m], send_sem.at[e], recv_sem.at[e], {"mp": to}).start()
 
-        partners(act, lo, hi)
-        if lo == 0:
-            dst[m] = src[m]
+        partners(act)
+        dst[m] = src[m]
+
+    def send_last(lo, hi):
+        @pl.loop(lo, hi)
+        def _(i):
+            far = (DEPTH - i) // 2
+            zt = (z + DEPTH + far * (1 - 2 * (i % 2))) % DEPTH
+            slot = i + 2 * (i % 2) - (2 if hi <= FAR + 1 else 1)
+            for base in bases:
+                put_last(base + 2 * zt, slot, 3 if hi <= FAR + 1 else 4)
+
+    def put_last(to, slot, e):
+        remote(
+            s4.at[to], r4.at[slot * plane + yc], send_sem.at[3], recv_sem.at[e], {"mp": to}
+        ).start()
+
+    def reorder(dst, src, lo, hi, into):
+        for j in range(lo, hi):
+            for y in range(plane // 2):
+                here = pl.ds(j * plane + 2 * y, 2)
+                there = pl.ds(y * (2 * DEPTH) + 2 * slot_z[j], 2)
+                if into:
+                    dst[here, :] = src[there, :]
+                else:
+                    dst[there, :] = src[here, :]
 
     def whole(e, src, dst):
         part = pl.ds(0, n - 1)
@@ -191,7 +222,9 @@
     loads[5].wait()
     ut_ref[...] = u_ref[...].T
     dt_ref[...] = d_ref[...].T
-    w1t_ref[...] = w1_ref[...].T
+    acc_ref[...] = w1_ref[...].astype(F32).T
+    reorder(rel_ref, acc_ref, 0, DEPTH, True)
+    w1t_ref[...] = rel_ref[...].astype(BF)
 
     half = tokens // 2
     whole(0, s1, r1).wait_recv()
@@ -204,10 +237,18 @@
         up = 0.5 * (1.0 + th)
         hid = (a * up).astype(BF)
         hid_ref[:, cols] = hid
-        slope_ref[:, cols] = up + (0.5 * a) * (1.0 - th * th) * (C0 + (3.0 * C0 * C1) * sq)
+        slope_ref[:, cols] = a
+        th_ref[:, cols] = th
         mid_ref[:, cols] = dot(dt_ref[...], hid, 1, 0).astype(BF)
     s3[...] = mid_ref[...].reshape(blocks)
     send_all(2, s3, r3)
+
+    for q in range(2):
+        cols = pl.ds(q * half, half)
+        a, th = slope_ref[:, cols], th_ref[:, cols]
+        slope_ref[:, cols] = 0.5 * (1.0 + th) + (0.5 * a) * (1.0 - th * th) * (
+            C0 + (3.0 * C0 * C1) * (a * a)
+        )
 
     whole(1, s2, r2).wait_recv()
     gcol_ref[...] = r2[...].reshape(flat)
@@ -219,10 +260,14 @@
         gp = (gh * slope_ref[:, cols]).astype(BF)
         gp_ref[:, cols] = gp
         mid_ref[:, cols] = dot(u_ref[...], gp, 1, 0).astype(BF)
+    s4[...] = mid_ref[...].reshape(blocks)
+    for base in bases:
+        put_last(base + 2 * slot_z[FAR], FAR, 4)
+    r4[(DEPTH - 1) * plane + yc] = s4[m]
+    send_last(1, 3)
     tu[...] = dot(col_ref[...], gp_ref[...], 1, 1).astype(BF).reshape(tu.shape)
     send_dp(0, tu, ru, True)
-    s4[...] = mid_ref[...].reshape(blocks)
-    send_all(3, s4, r4, 0, 8)
+    send_last(3, 9)
     ru[p] = tu[p]
     rd[p] = td[p]
     whole_dp(0, ru).wait()
@@ -231,7 +276,10 @@
     ad[p] = added(rd).astype(BF)
     send_dp(3, au.at[p], au, False)
     send_dp(4, ad.at[p], ad, False)
-    send_all(3, s4, r4, 8)
+    send_last(9, FAR + 1)
+    send_last(FAR + 1, DEPTH - 1)
+    for base in bases[:-1]:
+        put_last(base + 2 * z, DEPTH - 1, 4)
 
 
     whole(2, s3, r3).wait_recv()
@@ -244,29 +292,43 @@
     store_out(0, mixed_v, mixed_ref)
 
 
+    early = FAR * plane
+    first_part = r4.at[pl.ds(0, early)]
+    remote(first_part, first_part, send_sem.at[3], recv_sem.at[3], {"mp": (m + 1) % n}).wait_recv()
+    rows = r4[:early].reshape(early, tokens)
+    t_oi[...] = dot(rows, x_ref[...], 1, 0).astype(BF)
+    send_dp(5, t_oi, r_oi, False)
+    r_oi[p] = t_oi[...]
+
     whole_dp(2, r_oo).wait()
     w2g_v[...] = added(r_oo) * factor
     store_out(5, w2g_v, w2g_ref)
+    whole(0, s1, r1).wait_send()
+    whole(1, s2, r2).wait_send()
+    whole(2, s3, r3).wait_send()
     whole_dp(3, au).wait()
     ug_v[...] = au[...].astype(F32).reshape(ug_ref.shape) * factor
     store_out(3, ug_v, ug_ref)
     whole_dp(4, ad).wait()
     dg_v[...] = ad[...].astype(F32).reshape(dg_ref.shape) * factor
     store_out(4, dg_v, dg_ref)
-    whole(0, s1, r1).wait_send()
-    whole(1, s2, r2).wait_send()
-    whole(2, s3, r3).wait_send()
-
-    whole(3, s4, r4).wait_recv()
-    rows = r4[...].reshape(flat)
-    t_oi[...] = dot(rows, x_ref[...], 1, 0).astype(BF)
-    send_dp(5, t_oi, r_oi, False)
-    r_oi[p] = t_oi[...]
-    igrad_v[...] = dot(rows, w1t_ref[...], 0, 0).astype(BF)
+
+    last_part = r4.at[pl.ds(early, n - 1 - early)]
+    remote(last_part, last_part, send_sem.at[3], recv_sem.at[4], {"mp": (m + 1) % n}).wait_recv()
+    rows = r4[early:].reshape(n - early, tokens)
+    t_oj[...] = dot(rows, x_ref[...], 1, 0).astype(BF)
+    send_dp(6, t_oj, r_oj, False)
+    r_oj[p] = t_oj[...]
+    igrad_v[...] = dot(r4[...].reshape(flat), w1t_ref[...], 0, 0).astype(BF)
     store_out(1, igrad_v, igrad_ref)
+    whole_dp(5, r_oi).wait()
+    rel_ref[:early] = added(r_oi) * factor
+    reorder(acc_ref, rel_ref, 0, FAR, False)
     whole(3, s4, r4).wait_send()
-    whole_dp(5, r_oi).wait()
-    w1g_v[...] = added(r_oi).T * factor
+    whole_dp(6, r_oj).wait()
+    rel_ref[early:] = added(r_oj) * factor
+    reorder(acc_ref, rel_ref, FAR, DEPTH, False)
+    w1g_v[...] = acc_ref[...].T
     store_out(2, w1g_v, w1g_ref)
     for c in outs:
         c.wait()
@@ -293,6 +355,7 @@
     shape = jax.ShapeDtypeStruct
     vm = pltpu.VMEM
     lanes = t // 128
+    early = FAR * (n // DEPTH)
     blocks = vm((n, lanes, 128), BF)
     outs = pl.pallas_call(
         functools.partial(kernel, n, nd, float(t * nd) ** -0.5),
@@ -316,11 +379,14 @@
             vm((h, n), BF),
             vm((n, h), BF),
             vm((n, k), BF),
+            vm((n, k), F32),
+            vm((n, k), F32),
         ]
         + [blocks] * 8
         + [
             vm((n, t), BF),
             vm((n, t), BF),
+            vm((h, t), F32),
             vm((h, t), F32),
             vm((h, t), BF),
             vm((h, t), BF),
@@ -333,13 +399,15 @@
             vm((nd, h // nd, n), BF),
             vm((n, k), BF),
             vm((nd, n, k), BF),
-            vm((n, k), BF),
-            vm((nd, n, k), BF),
+            vm((early, k), BF),
+            vm((nd, early, k), BF),
+            vm((n - early, k), BF),
+            vm((nd, n - early, k), BF),
             pltpu.SemaphoreType.DMA((6,)),
             pltpu.SemaphoreType.DMA((4,)),
-            pltpu.SemaphoreType.DMA((4,)),
-            pltpu.SemaphoreType.DMA((6,)),
-            pltpu.SemaphoreType.DMA((6,)),
+            pltpu.SemaphoreType.DMA((5,)),
+            pltpu.SemaphoreType.DMA((7,)),
+            pltpu.SemaphoreType.DMA((7,)),
             pltpu.SemaphoreType.DMA((6,)),
             vm((t, k), BF),
             vm((t, k), BF),

time: 53.9 us -> 53.4 us (level)
  no operation moved by 1% of the time
where the time goes in v4:
time: 53.4 us; the launch traced here: 53.2 us
  Pallas kernels  52.6 us (99%)
  between operations  0.64 us (1%)
    pallas_call x1, Pallas kernels, local(): pl.pallas_call(functools.partial(kernel, n, nd, float(t * nd) ** (-0.5)),...  50.6 us
    pallas_call x1, Pallas kernels, local(): pl.pallas_call(store, out_shape=tuple((shape(o.shape, o.dtype) for o in o...  2.02 us

profile of v4, /device:TPU:1, one launch (start us, length us, event | category | flops | bytes accessed | tf_op | source)
XLA Modules:
  0.0 53.2 jit_solution(15370770442568049863)
XLA Ops:
  0.6 50.6 %shard_map.109 = (bf16[512,128]{1,0:T(8,128)(2,1)}, bf16[512,128]{1,0:T(8,128)(2,1)}, f32[128,128]{1,0:T(8,128)}, f32[128,512]{1,0:T(8,128)}, f32[512,128]{1,0:T(8,128)}, /*index=5*/f32[128,128]{1,0:T(8,128)}) custom-call(bf16[512,128]{1,0:T(8,128)(2,1)} %bitcast.12, bf16[512,128]{1,0:T(8,128)(2,1)} %bitcast.13, bf16[128,128]{1,0:T(8,128)(2,1)} %bitcast.16, ...), custom_call_target="tpu_custom_call" | custom-call | tf_op jit(solution)/shard_map/pallas_call | solution.py:360
  51.2 2.0 %shard_map.110 = (bf16[512,128]{1,0:T(8,128)(2,1)}, bf16[512,128]{1,0:T(8,128)(2,1)}, f32[128,128]{1,0:T(8,128)}, f32[128,512]{1,0:T(8,128)}, f32[512,128]{1,0:T(8,128)}, /*index=5*/f32[128,128]{1,0:T(8,128)}) custom-call(bf16[512,128]{1,0:T(8,128)(2,1)} %get-tuple-element.18.refs_0_, bf16[512,128]{1,0:T(8,128)(2,1)} %get-tuple-element.19.refs_1_, ...), custom_call_target="tpu_custom_call" | custom-call | tf_op jit(solution)/shard_map/pallas_call | solution.py:423
